TPU v7x, 512 devices: a whole 4x8x8 slice. The times are simulated.
512 devices in a mesh: dp: 16 (over y, core), seq: 32 (over x, z).
Axes of the slice: x: 4, y: 8, z: 8, core: 2. Of those that a mesh axis runs over, the one named last changes fastest.
Arguments:
- tokens: bfloat16 [8192, 4096], P('seq', 'dp'), may hold values from -6 to 6
- mask_flags: int32 [8192], P('seq'), may hold values 0 or 1
- doc_lengths: int32 [64], replicated, may hold values from 1 to 6144, 8192 in all
- mask_embed: bfloat16 [4096], P('dp'), may hold values from -6 to 6
- norm_gain: bfloat16 [4096], replicated, may hold values from 0.099609375 to 1.8984375
- qkv_weight: bfloat16 [4096, 16, 384], P(None, 'dp'), may hold values from -0.09375 to 0.09375
- out_weight: bfloat16 [16, 128, 4096], P('dp'), may hold values from -0.1875 to 0.1875
Outputs:
- mixed: bfloat16 [8192, 4096], P('seq', 'dp')
Inputs may be any that keep to these rules, and one draw needn't show every extreme that they name: `doc_lengths`: document lengths sum to 8192; the longest has exactly 6144 tokens.
All inputs are finite; a program needn't handle non-finite values. No bound on the sum of `mask_flags` on one device may be relied on, other than what follows from the above.
Results may differ from a plain program's by a relative error of at most 0.0045.
The roundings to bfloat16 on the way count: a program that leaves them out, or rounds other values in their place, can miss the bound.
Values may be sent and summed in bfloat16 or wider, within the bound.
A program may use at most 64 MiB of HBM per device.

v0:
```python
import math

import jax
import jax.numpy as jnp
from jax import lax
from jax.sharding import PartitionSpec as P


def segments_of(position, doc_ends):
    return jnp.sum((position[:, None] >= doc_ends[None, :]).astype(jnp.int32), axis=1)


def body(tokens, mask_flags, doc_lengths, mask_embed, norm_gain, qkv_weight, out_weight):
    row_count = tokens.shape[0]
    model_width = qkv_weight.shape[0]
    heads_here = qkv_weight.shape[1]
    head_size = out_weight.shape[1]
    masked = jnp.where(mask_flags[:, None] == 1, mask_embed[None, :], tokens)
    weight_flat = qkv_weight.reshape(model_width, heads_here * 3 * head_size)
    gain_values = norm_gain.astype(jnp.float32)
    piece_values = lax.all_gather(masked, "dp", axis=1, tiled=True).astype(jnp.float32)
    scaled = (piece_values * gain_values[None, :]).astype(jnp.bfloat16)
    running = jnp.dot(scaled, weight_flat, preferred_element_type=jnp.float32)
    squares = jnp.sum(piece_values * piece_values, axis=1, keepdims=True)
    running, squares = (running, squares)
    inv_rms = lax.rsqrt(squares / model_width + 1e-05)
    projected = (
        (running * inv_rms).astype(jnp.bfloat16).reshape(row_count, heads_here, 3, head_size)
    )
    queries = projected[:, :, 0, :]
    key_rows = projected[:, :, 1, :]
    value_rows = projected[:, :, 2, :]
    my_index = lax.axis_index("seq")
    doc_ends = jnp.cumsum(doc_lengths)
    row_start = my_index * row_count
    query_segment = segments_of(row_start + jnp.arange(row_count, dtype=jnp.int32), doc_ends)
    factor = 1.0 / math.sqrt(head_size)
    valid = jnp.bool_(True)
    key_piece = lax.all_gather(key_rows, "seq", axis=0, tiled=True)
    value_piece = lax.all_gather(value_rows, "seq", axis=0, tiled=True)
    key_count = key_piece.shape[0]
    key_segment = segments_of(jnp.arange(key_count, dtype=jnp.int32), doc_ends)
    scores = (
        jnp.einsum("qhd,khd->hqk", queries, key_piece, preferred_element_type=jnp.float32) * factor
    )
    same_doc = (query_segment[:, None] == key_segment[None, :]) & valid
    weights = jnp.where(same_doc[None], jnp.exp(scores), 0.0)
    numer_next = jnp.einsum(
        "hqk,khd->qhd",
        weights.astype(jnp.bfloat16),
        value_piece,
        preferred_element_type=jnp.float32,
    )
    denominator = jnp.sum(weights, axis=2).T
    attended = (numer_next / denominator[:, :, None]).astype(jnp.bfloat16)
    partial_value = jnp.einsum(
        "qhd,hdn->qn", attended, out_weight, preferred_element_type=jnp.float32
    )
    mixed = lax.psum_scatter(partial_value, "dp", scatter_dimension=1, tiled=True)
    return mixed.astype(jnp.bfloat16)


def solution(mesh):
    placed = (P("seq", "dp"), P("seq"), P(), P("dp"), P(), P(None, "dp", None), P("dp", None, None))
    return jax.shard_map(
        body, mesh=mesh, in_specs=placed, out_specs=P("seq", "dp"), check_vma=False
    )
```

profile of v0, /device:TPU:1, one launch (start us, length us, event | category | flops | bytes accessed | tf_op | source)
XLA Modules:
  0.0 306.2 jit_solution(6478012716378071951)
XLA Ops:
  6.5 0.0 copy-start
  6.5 0.0 all-gather.6.cloned.1.call-start
  6.5 0.8 broadcast_compare_fusion
  7.4 1.8 broadcast_select_fusion
  9.2 0.0 all-gather.6.cloned.1.call-update
  9.2 0.0 all-gather.10.cloned.1.call-start
  9.2 0.7 convert_element_type.32
  9.9 48.8 %all-gather.6.cloned.1.call-done = bf16[256,4096]{1,0:T(8,128)(2,1)} async-done(((bf16[256,256]{1,0:T(8,128)(2,1)}), bf16[256,4096]{1,0:T(8,128)(2,1)}) %all-gather.6.cloned.1.call-update) | async-done | bytes 2097168 | tf_op jit(solution)/shard_map/all_gather | solution.py:21
  58.7 2.1 fusion.3
  60.8 0.0 copy-done
  60.8 0.0 copy-start.1
  60.8 2.9 fusion.17
  63.7 0.1 copy.14
  63.9 0.6 fusion.49
  64.5 0.0 all-gather.10.cloned.1.call-update
  64.5 0.0 all-gather.8.cloned.1.call-start
  64.6 0.7 all-gather.8.cloned.1.call-update
  65.3 0.0 reduce-scatter.2.cloned.1.call-start
  65.3 0.0 copy-done.1
  65.3 0.1 copy.16
  65.4 0.1 reduce-window.8
  65.5 0.1 reduce.2
  65.6 0.1 convert_reduce_fusion.1
  65.7 0.3 convert_reduce_fusion
  66.1 75.5 %all-gather.10.cloned.1.call-done = bf16[8192,1,1,128]{0,3,2,1:T(8,128)(2,1)} async-done(((bf16[256,1,1,128]{0,3,2,1:T(8,128)(2,1)}), bf16[8192,1,1,128]{0,3,2,1:T(8,128)(2,1)}) %all-gather.10.cloned.1.call-update) | async-done | bytes 2097168 | tf_op jit(solution)/shard_map/all_gather | solution.py:39
  141.5 5.7 %fusion.50 = (f32[256]{0:T(256)S(1)}, bf16[256,8192]{1,0:T(8,128)(2,1)}) fusion(bf16[8192,1,1,128]{0,3,2,1:T(8,128)(2,1)} %all-gather.10.cloned.1.call-done, bf16[256,1,3,128]{0,3,2,1:T(8,128)(2,1)S(1)} %bitcast.56, s32[8192]{0:T(1024)S(1)} %convert_reduce_fusion, s32[256]{0:T(256)S(1)} %convert_reduce_fusion.1), kind=kOutput, calls=%fused_computation.32 | convolution fusion | flops 547356416 | bytes 6391808 | tf_op jit(solution)/shard_map/qhd,khd->hqk/dot_general | solution.py:44
  147.2 77.3 %all-gather.8.cloned.1.call-done = bf16[8192,1,1,128]{0,3,2,1:T(8,128)(2,1)} async-done(((bf16[256,1,1,128]{0,3,2,1:T(8,128)(2,1)}), bf16[8192,1,1,128]{0,3,2,1:T(8,128)(2,1)}) %all-gather.8.cloned.1.call-update) | async-done | bytes 2097168 | tf_op jit(solution)/shard_map/all_gather | solution.py:40
  224.6 8.1 %fusion.44 = f32[256,4096]{1,0:T(8,128)} fusion(bf16[256,8192]{1,0:T(8,128)(2,1)} %get-tuple-element.8, bf16[8192,1,1,128]{0,3,2,1:T(8,128)(2,1)} %all-gather.8.cloned.1.call-done, bf16[1,128,4096]{2,1,0:T(8,128)(2,1)} %param.13, f32[256]{0:T(256)S(1)} %get-tuple-element.7), kind=kOutput, calls=%fused_computation.22 | convolution fusion | flops 805371904 | bytes 11535360 | tf_op jit(solution)/shard_map/qhd,hdn->qn/dot_general | solution.py:56
  232.7 0.0 reduce-scatter.2.cloned.1.call-update
  232.7 65.3 %reduce-scatter.2.cloned.1.call-done = f32[256,256]{1,0:T(8,128)} async-done(((f32[256,4096]{1,0:T(8,128)}), f32[256,256]{1,0:T(8,128)}) %reduce-scatter.2.cloned.1.call-update) | async-done | bytes 262160 | tf_op jit(solution)/shard_map/reduce_scatter | solution.py:59
  298.1 1.6 convert_element_type.40
  (2 shorter events, 0.0 us)
Async XLA Ops:
  6.5 54.3 %copy-start = (bf16[4096,1,384]{2,0,1:T(8,128)(2,1)S(1)}, bf16[4096,1,384]{2,0,1:T(8,128)(2,1)}, u32[]{:S(2)}) copy-start(bf16[4096,1,384]{2,0,1:T(8,128)(2,1)} %param.12) | copy-start | bytes 9437188
  6.5 52.2 %all-gather.6.cloned.1.call-start = ((), (), s32[]{:S(2)}) async-start(), calls=%async_computation.1 | async-start | bytes 2228224 | tf_op jit(solution)/shard_map/all_gather | solution.py:21
  9.2 132.4 %all-gather.10.cloned.1.call-start = ((), (), s32[]{:S(2)}) async-start(), calls=%async_computation.4 | async-start | bytes 2162688 | tf_op jit(solution)/shard_map/all_gather | solution.py:39
  60.8 4.5 %copy-start.1 = (s32[64]{0:T(128)S(1)}, s32[64]{0:T(128)}, u32[]{:S(2)}) copy-start(s32[64]{0:T(128)} %param.9) | copy-start | bytes 772
  64.5 160.0 %all-gather.8.cloned.1.call-start = ((), (), s32[]{:S(2)}) async-start(), calls=%async_computation.3 | async-start | bytes 2162688 | tf_op jit(solution)/shard_map/all_gather | solution.py:40
  65.3 232.8 %reduce-scatter.2.cloned.1.call-start = ((), (), s32[]{:S(2)}) async-start(), calls=%async_computation.2 | async-start | bytes 4456448 | tf_op jit(solution)/shard_map/reduce_scatter | solution.py:59
Sparse Core Ops, SparseCore 0:
  9.4 49.2 all-gather.5
  64.6 76.8 all-gather.9
  144.6 79.9 all-gather.7
  232.8 65.1 reduce-scatter.1
where the time goes:
time: 308 us; the launch traced here: 306 us
  waiting for transfers between devices  268 us (87%)
  matrix products  16.7 us (5%)
  between operations  13.2 us (4%)
  other arithmetic  7.67 us (2%)
    all_gather x1, waiting for transfers between devices, body(): value_piece = lax.all_gather(value_rows, 'seq', axis=0, tiled=True)  77.3 us
    all_gather x1, waiting for transfers between devices, body(): key_piece = lax.all_gather(key_rows, 'seq', axis=0, tiled=True)  75.5 us
    reduce_scatter x1, waiting for transfers between devices, body(): lax.psum_scatter(partial_value, 'dp', scatter_dimension=1, tiled=True)  65.3 us
    all_gather x1, waiting for transfers between devices, body(): lax.all_gather(masked, 'dp', axis=1, tiled=True).astype(jnp.float32)  48.8 us
    dot_general x1, matrix products, body(): jnp.einsum('qhd,hdn->qn', attended, out_weight, preferred_element_type=jn...  8.14 us
  transfers between devices with their start and end apart: 4, of which 4 were waited for; matrix products, arithmetic and copies ran while one was open for 2% of the time, Pallas kernels for 0%

commit v1 on v0

v1 whole, which is shorter than its diff:
```python
import math

import jax
import jax.numpy as jnp
from jax import lax
from jax.experimental import pallas as pl
from jax.experimental.pallas import tpu as pltpu
from jax.sharding import PartitionSpec as P

NY, NX, NZ = 8, 4, 8
ROWS, FEAT, HD, HEADS, D = 256, 256, 128, 16, 4096
NC = 2
R = ROWS // NC
H = R // 2
F32, BF16 = jnp.float32, jnp.bfloat16
SCALE = math.log2(math.e) / math.sqrt(HD)


def remote(src, dst, send, recv, dp, seq):
    return pltpu.make_async_remote_copy(
        src_ref=src, dst_ref=dst, send_sem=send, recv_sem=recv,
        device_id=(dp, seq), device_id_type=pl.DeviceIdType.MESH,
    )


class Ring:
    def __init__(self, slot, send, recv, up, down, c):
        self.slot, self.send, self.recv, self.up, self.down, self.c = slot, send, recv, up, down, c
        self.copies = {}

    def go(self, direction, s):
        to = s + 1 if direction == "up" else (s - 1) % 8
        half = None
        if to == 4:
            half = 0 if direction == "up" else 1
        sem = 8 if to == 4 and direction == "down" else to
        copy = remote(
            self.slot(s, half), self.slot(to, half), self.send.at[self.c, sem], self.recv.at[self.c, sem],
            *(self.up if direction == "up" else self.down),
        )
        copy.start()
        self.copies[sem] = copy

    def arrived(self, direction, t):
        sem = t if direction == "up" else (8 if t == 4 else 8 - t)
        self.copies[sem].wait_recv()

    def finish(self):
        for copy in self.copies.values():
            copy.wait_send()


class Pair:
    def __init__(self, mine, theirs, send, recv, other, c):
        self.mine, self.theirs, self.send, self.recv, self.other, self.c = mine, theirs, send, recv, other, c
        self.copies = {}

    def go(self, s):
        copy = remote(self.mine(s), self.theirs(s), self.send.at[self.c, s], self.recv.at[self.c, s], *self.other)
        copy.start()
        self.copies[s] = copy

    def arrived(self, s):
        self.copies[s].wait_recv()

    def finish(self):
        for copy in self.copies.values():
            copy.wait_send()


def kernel(
    tokens, flags, lens, embed, gain, wqkv, wout, out,
    tokin, tok, w, kv, q, numer, den, redo, redi, att, wb, acc, ssq, segq, segk,
    local, ysend, yrecv, bsend, brecv, zsend, zrecv, qsend, qrecv, rsend, rrecv,
    asend, arecv, csend, crecv, was, war, wbs, wbr, wcs, wcr,
):
    dp, seq = lax.axis_index("dp"), lax.axis_index("seq")
    y, core = dp // 2, lax.rem(dp, 2)
    x, z = seq // NZ, lax.rem(seq, NZ)

    load_tok = pltpu.make_async_copy(tokens, tokin, local.at[0])
    load_w = pltpu.make_async_copy(wqkv, w, local.at[1])
    load_tok.start()
    load_w.start()

    def dp_at(dy, c):
        return lax.rem(y + dy + NY, NY) * 2 + c

    def seq_at(dx, dz):
        return lax.rem(x + dx + NX, NX) * NZ + lax.rem(z + dz + NZ, NZ)

    barrier = pltpu.get_barrier_semaphore()

    @pl.loop(1, HEADS)
    def _(k):
        pl.semaphore_signal(
            barrier, inc=1, device_id=(lax.rem(dp + k, HEADS), seq), device_id_type=pl.DeviceIdType.MESH
        )

    @pl.loop(1, NZ)
    def _(k):
        pl.semaphore_signal(barrier, inc=1, device_id=(dp, seq_at(0, k)), device_id_type=pl.DeviceIdType.MESH)

    @pl.loop(1, NX)
    def _(k):
        pl.semaphore_signal(barrier, inc=1, device_id=(dp, seq_at(k, 0)), device_id_type=pl.DeviceIdType.MESH)

    load_tok.wait()
    embed_row = embed[...].astype(F32)
    for c in range(NC):
        rows = pl.ds(c * R, R)
        flag = jnp.transpose(jnp.broadcast_to(flags[c : c + 1, :].astype(F32), (R, R)))
        flag = jnp.concatenate([flag, flag], axis=1)
        masked = jnp.where(flag == 1.0, embed_row, tokin[rows, :].astype(F32))
        tok[0, 0, rows, :] = masked.astype(BF16)

    pl.semaphore_wait(barrier, HEADS - 1 + NZ - 1 + NX - 1)

    up_y, down_y = (dp_at(1, core), seq), (dp_at(-1, core), seq)
    up_z, down_z = (dp, seq_at(0, 1)), (dp, seq_at(0, -1))
    sibling = (y * 2 + 1 - core, seq)

    def part(c, half):
        return pl.ds(c * R, R) if half is None else pl.ds(c * R + half * H, H)

    token_ring = [
        Ring(lambda s, half, c=c: tok.at[0, s, part(c, half)], ysend, yrecv, up_y, down_y, c) for c in range(NC)
    ]
    token_pair = [
        Pair(lambda s, c=c: tok.at[0, s, part(c, None)], lambda s, c=c: tok.at[1, s, part(c, None)],
             bsend, brecv, sibling, c) for c in range(NC)
    ]
    kv_ring = [
        Ring(lambda s, half, c=c: kv.at[s, part(c, half)], zsend, zrecv, up_z, down_z, c) for c in range(NC)
    ]
    att_ring = [
        Ring(lambda s, half, c=c: att.at[0, s, part(c, half)], asend, arecv, up_y, down_y, c) for c in range(NC)
    ]
    att_pair = [
        Pair(lambda s, c=c: att.at[0, s, part(c, None)], lambda s, c=c: att.at[1, s, part(c, None)],
             csend, crecv, sibling, c) for c in range(NC)
    ]

    def own_tokens(c):
        token_ring[c].go("up", 0)
        token_ring[c].go("down", 0)

    own_tokens(0)
    for c in range(NC):
        token_pair[c].go(0)

    holder = lax.rem(dp, NX) == x
    hq = dp // NX

    def out_tile(d):
        return wout.at[0, pl.ds(pl.multiple_of(z * 16, 16), 16), pl.ds(pl.multiple_of(d * FEAT, FEAT), FEAT)]

    def first_hop(k):
        d = lax.rem(dp + k, HEADS)
        return remote(out_tile(d), wb.at[x, z, hq], was.at[k], war.at[hq], d, seq)

    own_tile = pltpu.make_async_copy(out_tile(dp), wb.at[x, z, hq], local.at[2])

    @pl.when(holder)
    def _():
        own_tile.start()

        @pl.loop(1, HEADS)
        def _(k):
            first_hop(k).start()

    def second_hop(k):
        return remote(wb.at[x, z], wb.at[x, z], wbs.at[k], wbr.at[k], dp, seq_at(0, k))

    def third_hop(k):
        return remote(wb.at[x], wb.at[x], wcs.at[k], wcr.at[k], dp, seq_at(k, 0))

    def start_second():
        @pl.when(holder)
        def _():
            own_tile.wait()

        @pl.loop(0, HEADS // NX)
        def _(i):
            @pl.when(i * NX + x != dp)
            def _():
                remote(
                    out_tile(dp), wb.at[x, z, i], was.at[0], war.at[i], lax.rem(dp + 1, HEADS), seq
                ).wait_recv()

        @pl.loop(1, NZ)
        def _(k):
            second_hop(k).start()

    def start_third():
        @pl.loop(1, NZ)
        def _(k):
            second_hop(k).wait_recv()

        @pl.loop(1, NX)
        def _(k):
            third_hop(k).start()

    lane = lax.broadcasted_iota(jnp.int32, (HD, HD), 1)
    row = lax.broadcasted_iota(jnp.int32, (HD, HD), 0)
    lens_lane = jnp.broadcast_to(lens[...].astype(F32), (HD, HD))
    lens_row = jnp.transpose(lens_lane)
    ends_lane = jnp.sum(jnp.where(row <= lane, lens_row, 0.0), axis=0, keepdims=True)
    ends_row = jnp.sum(jnp.where(lane <= row, lens_lane, 0.0), axis=1, keepdims=True)
    for s in range(NX):
        base = seq_at(-s, 0) * ROWS
        position = (lax.broadcasted_iota(jnp.int32, (ROWS, HD), 0) + base).astype(F32)
        count = jnp.sum(jnp.where(position >= ends_lane, 1.0, 0.0), axis=1, keepdims=True)
        segq[s] = jnp.broadcast_to(count, (ROWS, HD))
    for s in range(NZ):
        base = seq_at(0, -s) * ROWS
        position = (lax.broadcasted_iota(jnp.int32, (HD, ROWS), 1) + base).astype(F32)
        count = jnp.sum(jnp.where(position >= ends_row, 1.0, 0.0), axis=0, keepdims=True)
        segk[s] = jnp.broadcast_to(count, (8, ROWS))

    numer[...] = jnp.zeros_like(numer)
    den[...] = jnp.zeros_like(den)
    load_w.wait()

    def project(o, s, c):
        rows = pl.ds(c * R, R)
        f = dp_at(-s, core if o == 0 else 1 - core)
        values = tok[o, s, rows, :].astype(F32)
        squares = values * values
        squares = squares[:, :HD] + squares[:, HD:]
        scaled = (values * gain[pl.ds(f, 1), :]).astype(BF16)
        product = jnp.dot(
            scaled, w[pl.ds(pl.multiple_of(f * FEAT, FEAT), FEAT), :], preferred_element_type=F32
        )
        if (o, s) == (0, 0):
            ssq[rows, :] = squares
            acc[rows, :] = product
        else:
            ssq[rows, :] += squares
            acc[rows, :] += product

    q_copies = {}

    def projected(c):
        rows = pl.ds(c * R, R)
        total = jnp.sum(ssq[rows, :], axis=1, keepdims=True)
        inv_rms = lax.rsqrt(total / D + 1e-05)
        values = (acc[rows, :] * inv_rms).astype(BF16)
        kv[0, rows, :] = values[:, HD:]
        q[0, rows, :] = values[:, :HD]
        kv_ring[c].go("up", 0)
        kv_ring[c].go("down", 0)
        for k in range(1, NX):
            copy = remote(q.at[0, rows], q.at[k, rows], qsend.at[c, k], qrecv.at[c, k], dp, seq_at(k, 0))
            copy.start()
            q_copies[c, k] = copy

    def attend(qc, s, c):
        rows = pl.ds(qc * R, R)
        keys = pl.ds(c * R, R)
        queries = q[:, rows, :].reshape(NX * R, HD)
        scores = lax.dot_general(
            queries, kv[s, keys, :HD], (((1,), (1,)), ((), ())), preferred_element_type=F32
        )
        same = segq[:, rows, :].reshape(NX * R, HD) == segk[s, 0:1, keys]
        weights = jnp.where(same, jnp.exp2(scores * SCALE), 0.0)
        product = jnp.dot(weights.astype(BF16), kv[s, keys, HD:], preferred_element_type=F32)
        numer[:, rows, :] += product.reshape(NX, R, HD)
        den[:, rows, :] += weights.reshape(NX, R, HD)

    def token_step(c, t):
        ring, pair = token_ring[c], token_pair[c]
        if t == 0:
            project(0, 0, c)
            return
        ring.arrived("up", t)
        if t < 4:
            ring.go("up", t)
            pair.go(t)
        ring.arrived("down", t)
        if t < 4:
            ring.go("down", 8 - t)
            pair.go(8 - t)
        else:
            pair.go(4)
        project(0, t, c)
        if t < 4:
            project(0, 8 - t, c)
        pair.arrived(t - 1)
        project(1, t - 1, c)
        if t > 1:
            pair.arrived(9 - t)
            project(1, 9 - t, c)
        if t == 4:
            pair.arrived(4)
            project(1, 4, c)

    def kv_step(c, t, chunks):
        ring = kv_ring[c]
        if t == 0:
            for k in range(1, NX):
                q_copies[c, k].wait_recv()
        else:
            ring.arrived("up", t)
            if t < 4:
                ring.go("up", t)
            ring.arrived("down", t)
            if t < 4:
                ring.go("down", 8 - t)
        for qc in chunks:
            attend(qc, t, c)
            if 0 < t < 4:
                attend(qc, 8 - t, c)

    for c in range(NC):
        for t in range(5):
            token_step(c, t)
            if c > 0:
                kv_step(c - 1, t, [c - 1])
            if t == 2:
                if c + 1 < NC:
                    own_tokens(c + 1)
                if c == 0:
                    start_second()
                if c == 1:
                    start_third()
        projected(c)

    last = NC - 1
    for t in range(4):
        kv_step(last, t, range(NC))
        for c in range(last):
            attend(last, t, c)
            attend(last, t + 4, c)
    kv_step(last, 4, range(NC))

    r_copies = {}
    for k in (2, 1, 3):
        redo[k, :ROWS, :] = numer[k]
        for i in range(ROWS // HD):
            part_sum = jnp.sum(jnp.transpose(den[k, pl.ds(i * HD, HD), :]), axis=0, keepdims=True)
            redo[k, pl.ds(ROWS + 8 * i, 8), :] = jnp.broadcast_to(part_sum, (8, HD))
        copy = remote(redo.at[k], redi.at[k], rsend.at[k], rrecv.at[k], dp, seq_at(-k, 0))
        copy.start()
        r_copies[k] = copy
    for k in (1, 3, 2):
        r_copies[k].wait_recv()
    for c in range(NC):
        rows = pl.ds(c * R, R)
        down = jnp.sum(jnp.transpose(den[0, rows, :]), axis=0, keepdims=True)
        for k in range(1, NX):
            down = down + redi[k, pl.ds(ROWS + 8 * c, 8), :][0:1, :]
        down = jnp.transpose(jnp.broadcast_to(down, (HD, HD)))
        top = numer[0, rows, :] + redi[1, rows, :] + redi[2, rows, :] + redi[3, rows, :]
        att[0, 0, rows, :] = (top / down).astype(BF16)
        att_ring[c].go("up", 0)
        att_ring[c].go("down", 0)
        att_pair[c].go(0)

    @pl.loop(1, NX)
    def _(k):
        third_hop(k).wait_recv()

    def mix(o, s, c):
        rows = pl.ds(c * R, R)
        h = dp_at(-s, core if o == 0 else 1 - core)
        weight = wb[lax.rem(h, NX), :, h // NX].reshape(HD, FEAT)
        product = jnp.dot(att[o, s, rows, :], weight, preferred_element_type=F32)
        if (o, s) == (0, 0):
            acc[rows, :FEAT] = product
        else:
            acc[rows, :FEAT] += product

    for t in range(5):
        for c in range(NC):
            ring, pair = att_ring[c], att_pair[c]
            if t > 0:
                ring.arrived("up", t)
                if t < 4:
                    ring.go("up", t)
                    pair.go(t)
                ring.arrived("down", t)
                if t < 4:
                    ring.go("down", 8 - t)
                    pair.go(8 - t)
                else:
                    pair.go(4)
        for c in range(NC):
            pair = att_pair[c]
            mix(0, t, c)
            if 0 < t < 4:
                mix(0, 8 - t, c)
            if t > 0:
                pair.arrived(t - 1)
                mix(1, t - 1, c)
            if t > 1:
                pair.arrived(9 - t)
                mix(1, 9 - t, c)
            if t == 4:
                pair.arrived(4)
                mix(1, 4, c)
    out[...] = acc[:, :FEAT].astype(BF16)

    for c in range(NC):
        for group in (token_ring[c], token_pair[c], kv_ring[c], att_ring[c], att_pair[c]):
            group.finish()
    for copy in list(q_copies.values()) + list(r_copies.values()):
        copy.wait_send()

    @pl.when(holder)
    def _():
        @pl.loop(1, HEADS)
        def _(k):
            first_hop(k).wait_send()

    @pl.loop(1, NZ)
    def _(k):
        second_hop(k).wait_send()

    @pl.loop(1, NX)
    def _(k):
        third_hop(k).wait_send()


def body(tokens, mask_flags, doc_lengths, mask_embed, norm_gain, qkv_weight, out_weight):
    lens = jnp.pad(doc_lengths, (0, HD - doc_lengths.shape[0])).reshape(1, HD)
    vmem = pl.BlockSpec(memory_space=pltpu.VMEM)
    anyw = pl.BlockSpec(memory_space=pl.ANY)
    dma = lambda *shape: pltpu.SemaphoreType.DMA(shape)
    return pl.pallas_call(
        kernel,
        out_shape=jax.ShapeDtypeStruct((ROWS, FEAT), BF16),
        in_specs=[anyw, vmem, vmem, vmem, vmem, anyw, anyw],
        out_specs=vmem,
        scratch_shapes=[
            pltpu.VMEM((ROWS, FEAT), BF16),
            pltpu.VMEM((2, NY, ROWS, FEAT), BF16),
            pltpu.VMEM((D, 3 * HD), BF16),
            pltpu.VMEM((NZ, ROWS, 2 * HD), BF16),
            pltpu.VMEM((NX, ROWS, HD), BF16),
            pltpu.VMEM((NX, ROWS, HD), F32),
            pltpu.VMEM((NX, ROWS, HD), F32),
            pltpu.VMEM((NX, ROWS + 16, HD), F32),
            pltpu.VMEM((NX, ROWS + 16, HD), F32),
            pltpu.VMEM((2, NY, ROWS, HD), BF16),
            pltpu.VMEM((NX, NZ, HEADS // NX, 16, FEAT), BF16),
            pltpu.VMEM((ROWS, 3 * HD), F32),
            pltpu.VMEM((ROWS, HD), F32),
            pltpu.VMEM((NX, ROWS, HD), F32),
            pltpu.VMEM((NZ, 8, ROWS), F32),
            dma(3),
            dma(NC, 9), dma(NC, 9), dma(NC, 8), dma(NC, 8),
            dma(NC, 9), dma(NC, 9), dma(NC, NX), dma(NC, NX),
            dma(NX), dma(NX),
            dma(NC, 9), dma(NC, 9), dma(NC, 8), dma(NC, 8),
            dma(HEADS), dma(HEADS // NX), dma(NZ), dma(NZ), dma(NX), dma(NX),
        ],
        compiler_params=pltpu.CompilerParams(
            collective_id=0, has_side_effects=True, vmem_limit_bytes=48 * 1024 * 1024
        ),
        name="attention_layer",
    )(
        tokens, mask_flags.reshape(NC, R), lens, mask_embed.astype(F32).reshape(1, FEAT),
        norm_gain.astype(F32).reshape(HEADS, FEAT), qkv_weight.reshape(D, 3 * HD), out_weight,
    )


def solution(mesh):
    placed = (P("seq", "dp"), P("seq"), P(), P("dp"), P(), P(None, "dp", None), P("dp", None, None))
    return jax.shard_map(
        body, mesh=mesh, in_specs=placed, out_specs=P("seq", "dp"), check_vma=False
    )
```

time: 308 us -> 97.4 us (0.32)
  waiting for transfers between devices: 268 us -> 0 us
  Pallas kernels: 0 us -> 89.7 us
  matrix products: 16.7 us -> 0 us
  between operations: 13.2 us -> 0.02 us
  other arithmetic: 7.67 us -> 0.66 us
  local copies, waits for them, and re-layouts: 0.9 us -> 6.71 us
    all_gather x3 -> x0, waiting for transfers between devices: 202 us -> none  [the longest x1 77.3 us: body(): value_piece = lax.all_gather(value_rows, 'seq', axis=0, tiled=True)]
    pallas_call x0 -> x1, Pallas kernels: none -> 89.7 us  [body(): pl.pallas_call(kernel, out_shape=jax.ShapeDtypeStruct((ROWS, FEAT), BF16)...]
    reduce_scatter x1 -> x0, waiting for transfers between devices: 65.3 us -> none  [body(): lax.psum_scatter(partial_value, 'dp', scatter_dimension=1, tiled=True)]
    dot_general x3 -> x0, matrix products: 16.7 us -> none  [the longest x1 8.14 us: body(): jnp.einsum('qhd,hdn->qn', attended, out_weight, preferred_element_type=jn...]
    unnamed x4 -> x9, local copies, waits for them, and re-layouts: 0.01 us -> 5.35 us
  transfers between devices with their start and end apart: 4 -> 0, of which waited for: 4 -> 0; matrix products, arithmetic and copies ran while one was open for 2% -> 0% of each run, Pallas kernels for 0% -> 0%
where the time goes in v1:
time: 97.4 us; the launch traced here: 97.1 us
  Pallas kernels  89.7 us (92%)
  local copies, waits for them, and re-layouts  6.71 us (7%)
    pallas_call x1, Pallas kernels, body(): pl.pallas_call(kernel, out_shape=jax.ShapeDtypeStruct((ROWS, FEAT), BF16)...  89.7 us
    unnamed x9, local copies, waits for them, and re-layouts  5.35 us

profile of v1, /device:TPU:1, one launch (start us, length us, event | category | flops | bytes accessed | tf_op | source)
XLA Modules:
  0.0 97.1 jit_solution(11143046935743996010)
XLA Ops:
  0.0 0.7 pad_bitcast_fusion.lens
  0.7 0.7 reshape.26
  1.3 0.7 reshape.29.gain
  2.0 0.0 copy-start
  2.0 1.9 %copy-done = bf16[4096,1,384]{2,0,1:T(8,128)(2,1)S(1)} copy-done((bf16[4096,1,384]{2,0,1:T(8,128)(2,1)S(1)}, bf16[4096,1,384]{2,0,1:T(8,128)(2,1)}, u32[]{:S(2)}) %copy-start) | copy-done | bytes 3145752
  3.9 0.0 copy-start.1
  3.9 1.2 %copy-done.1 = bf16[1,128,4096]{2,1,0:T(8,128)(2,1)S(1)} copy-done((bf16[1,128,4096]{2,1,0:T(8,128)(2,1)S(1)}, bf16[1,128,4096]{2,1,0:T(8,128)(2,1)}, u32[]{:S(2)}) %copy-start.1) | copy-done | bytes 1048600
  5.1 0.0 copy-start.2
  5.1 0.9 copy-done.2
  6.0 0.0 copy-start.3
  6.0 0.7 copy-done.3
  6.7 89.7 %attention_layer.1 = bf16[256,256]{1,0:T(8,128)(2,1)S(1)} custom-call(bf16[256,256]{1,0:T(8,128)(2,1)S(1)} %copy-done.2, s32[2,128]{1,0:T(2,128)S(1)} %bitcast.6, s32[1,128]{1,0:T(1,128)S(1)} %pad_bitcast_fusion.lens, f32[1,256]{1,0:T(1,128)S(1)} %bitcast.7, f32[16,256]{1,0:T(8,128)S(1)} %reshape.29.gain, bf16[4096,384]{1,0:T(8,128)(2,1)S(1)} %bitcast.5, ...), custom_call_target="tpu_custom_call" | custom-call | tf_op jit(solution)/shard_map/attention_layer/pallas_call | solution.py:430
  96.5 0.7 copy.9
Async XLA Ops:
  2.0 1.9 %copy-start = (bf16[4096,1,384]{2,0,1:T(8,128)(2,1)S(1)}, bf16[4096,1,384]{2,0,1:T(8,128)(2,1)}, u32[]{:S(2)}) copy-start(bf16[4096,1,384]{2,0,1:T(8,128)(2,1)} %param.12) | copy-start | bytes 9437188
  3.9 1.2 %copy-start.1 = (bf16[1,128,4096]{2,1,0:T(8,128)(2,1)S(1)}, bf16[1,128,4096]{2,1,0:T(8,128)(2,1)}, u32[]{:S(2)}) copy-start(bf16[1,128,4096]{2,1,0:T(8,128)(2,1)} %wout.1) | copy-start | bytes 3145732
  5.1 0.9 copy-start.2
  6.0 0.7 copy-start.3

commit v2 on v0

v2 whole, which is shorter than its diff:
```python
import math

import jax
import jax.numpy as jnp
from jax import lax
from jax.experimental import pallas as pl
from jax.experimental.pallas import tpu as pltpu
from jax.sharding import PartitionSpec as P

NY, NX, NZ = 8, 4, 8
ROWS, FEAT, HD, HEADS, D, DOCS = 256, 256, 128, 16, 4096, 64
VMEM_BYTES = 63 * 1024 * 1024
H = ROWS // 2
F32, BF16 = jnp.float32, jnp.bfloat16
SCALE = math.log2(math.e) / math.sqrt(HD)


def remote(src, dst, send, recv, dp, seq):
    return pltpu.make_async_remote_copy(
        src_ref=src, dst_ref=dst, send_sem=send, recv_sem=recv,
        device_id=(dp, seq), device_id_type=pl.DeviceIdType.MESH,
    )


CROSS = ((0, 1), (0, -1), (1, 1), (3, -1))
TREE = ((0, 2), (0, -2), (0, 1), (0, -1), (2, 2), (6, -2), (2, 1), (6, -1))


T_PLAN = TREE
KV_PLAN = TREE
ATT_PLAN = TREE


class Ring:
    size = 8

    def __init__(self, plan, slot, send, recv, place):
        self.plan, self.slot, self.send, self.recv, self.place = plan, slot, send, recv, place
        self.copies = {}

    def go(self, s):
        for source, step in self.plan:
            if source == s:
                to = (s + step) % self.size
                half = None if to != self.size // 2 else (0 if step > 0 else 1)
                sem = self.size if half == 1 else to
                copy = remote(
                    self.slot(s, half), self.slot(to, half), self.send.at[sem], self.recv.at[sem],
                    *self.place(step),
                )
                copy.start()
                self.copies[sem] = copy

    def arrived(self, s):
        for sem in (s, self.size) if s == self.size // 2 else (s,):
            self.copies[sem].wait_recv()

    def finish(self):
        for sem, copy in self.copies.items():
            copy.wait_send()


class ShortRing(Ring):
    size = 4


class Pair:
    def __init__(self, mine, theirs, send, recv, other):
        self.mine, self.theirs, self.send, self.recv, self.other = mine, theirs, send, recv, other
        self.copies = {}

    def go(self, s):
        copy = remote(self.mine(s), self.theirs(s), self.send.at[s], self.recv.at[s], *self.other)
        copy.start()
        self.copies[s] = copy

    def arrived(self, s):
        self.copies[s].wait_recv()

    def finish(self):
        for sem, copy in self.copies.items():
            copy.wait_send()


def kernel(
    tokens, flags, lens, embed, gain, wqkv, wout, out,
    tokin, flagin, lenin, embedin, gainin, gain32, tok, w, kv, q, numer, den, redo, redi, dedo, dedi, att, wb, acc, ssq, segq, segk,
    local, ysend, yrecv, bsend, brecv, zsend, zrecv, qsend, qrecv, rsend, rrecv,
    asend, arecv, csend, crecv, was, war, wbs, wbr, wcs, wcr,
):
    dp, seq = lax.axis_index("dp"), lax.axis_index("seq")
    y, core = dp // 2, lax.rem(dp, 2)
    x, z = seq // NZ, lax.rem(seq, NZ)

    loads = [
        pltpu.make_async_copy(there, here, local.at[i])
        for i, (there, here) in enumerate(
            [(tokens, tokin), (flags, flagin), (embed, embedin), (gain, gainin), (lens, lenin), (wqkv, w)]
        )
    ]
    for load in loads:
        load.start()

    def dp_at(dy, c):
        return lax.rem(y + dy + NY, NY) * 2 + c

    def seq_at(dx, dz):
        return lax.rem(x + dx + NX, NX) * NZ + lax.rem(z + dz + NZ, NZ)

    barrier = pltpu.get_barrier_semaphore()

    @pl.loop(1, HEADS)
    def _(k):
        pl.semaphore_signal(
            barrier, inc=1, device_id=(lax.rem(dp + k, HEADS), seq), device_id_type=pl.DeviceIdType.MESH
        )

    @pl.loop(1, NZ)
    def _(k):
        pl.semaphore_signal(barrier, inc=1, device_id=(dp, seq_at(0, k)), device_id_type=pl.DeviceIdType.MESH)

    @pl.loop(1, NX)
    def _(k):
        pl.semaphore_signal(barrier, inc=1, device_id=(dp, seq_at(k, 0)), device_id_type=pl.DeviceIdType.MESH)

    for load in loads[:3]:
        load.wait()
    embed_row = jnp.concatenate([embedin[0:1, :], embedin[1:2, :]], axis=1).astype(F32)
    for c in range(ROWS // HD):
        rows = pl.ds(c * HD, HD)
        flag = jnp.transpose(jnp.broadcast_to(flagin[c : c + 1, :].astype(F32), (HD, HD)))
        flag = jnp.concatenate([flag, flag], axis=1)
        masked = jnp.where(flag == 1.0, embed_row, tokin[rows, :].astype(F32))
        tok[0, 0, rows, :] = masked.astype(BF16)

    pl.semaphore_wait(barrier, HEADS - 1 + NZ - 1 + NX - 1)

    def along_y(step):
        return dp_at(step, core), seq

    def along_z(step):
        return dp, seq_at(0, step)

    sibling = (y * 2 + 1 - core, seq)

    def along_x(step):
        return dp, seq_at(step, 0)

    def rows_of(half):
        return pl.ds(0, ROWS) if half is None else pl.ds(half * H, H)

    token_ring = Ring(T_PLAN, lambda s, half: tok.at[0, s, rows_of(half)], ysend, yrecv, along_y)
    token_pair = Pair(lambda s: tok.at[0, s], lambda s: tok.at[1, s], bsend, brecv, sibling)
    kv_ring = Ring(KV_PLAN, lambda s, half: kv.at[s, rows_of(half)], zsend, zrecv, along_z)
    att_ring = Ring(ATT_PLAN, lambda s, half: att.at[0, s, rows_of(half)], asend, arecv, along_y)
    att_pair = Pair(lambda s: att.at[0, s], lambda s: att.at[1, s], csend, crecv, sibling)

    def weight_part(s, half):
        return wb.at[s] if half is None else wb.at[s, pl.ds(half * (NZ // 2), NZ // 2)]

    weight_ring = ShortRing(CROSS, weight_part, wcs, wcr, along_x)

    turn = lax.rem(x - dp + HEADS, NX)

    def out_tile(d):
        return wout.at[0, pl.ds(pl.multiple_of(z * 16, 16), 16), pl.ds(pl.multiple_of(d * FEAT, FEAT), FEAT)]

    def first_hop(i):
        d = NX * i + turn
        return remote(out_tile(d), wb.at[0, z, dp // NX], was.at[i], war.at[dp // NX], d, seq)

    own_tile = pltpu.make_async_copy(out_tile(dp), wb.at[0, z, dp // NX], local.at[6])

    def second_hop(k):
        return remote(wb.at[0, z], wb.at[0, z], wbs.at[k], wbr.at[k], dp, seq_at(0, k))


    def start_first():
        for i in range(HEADS // NX):
            @pl.when(NX * i + turn != dp)
            def _():
                first_hop(i).start()

            @pl.when(NX * i + turn == dp)
            def _():
                own_tile.start()

    def finish_first():
        for i in range(HEADS // NX):
            @pl.when(NX * i + turn != dp)
            def _():
                remote(out_tile(dp), wb.at[0, z, i], was.at[i], war.at[i], NX * i + turn, seq).wait_recv()

            @pl.when(NX * i + turn == dp)
            def _():
                own_tile.wait()

    def start_second():
        finish_first()

        @pl.loop(1, NZ)
        def _(k):
            second_hop(k).start()

    def start_third():
        @pl.loop(1, NZ)
        def _(k):
            second_hop(k).wait_recv()

        weight_ring.go(0)

    def project(o, s):
        f = dp_at(-s, core if o == 0 else 1 - core)
        values = tok[o, s].astype(F32)
        squares = values * values
        squares = squares[:, :HD] + squares[:, HD:]
        gains = jnp.concatenate([gain32[pl.ds(2 * f, 1), :], gain32[pl.ds(2 * f + 1, 1), :]], axis=1)
        scaled = (values * gains).astype(BF16)
        product = jnp.dot(
            scaled, w[pl.ds(pl.multiple_of(f * FEAT, FEAT), FEAT), :], preferred_element_type=F32
        )
        if (o, s) == (0, 0):
            ssq[...] = squares
            acc[...] = product
        else:
            ssq[...] += squares
            acc[...] += product

    q_copies = {}

    def projected():
        total = jnp.sum(ssq[...], axis=1, keepdims=True)
        inv_rms = lax.rsqrt(total / D + 1e-05)
        kv[0] = (acc[:, HD:] * inv_rms).astype(BF16)
        kv_ring.go(0)
        q[0] = (acc[:, :HD] * inv_rms).astype(BF16)
        for k in (2, 1, 3):
            copy = remote(q.at[0], q.at[k], qsend.at[k], qrecv.at[k], dp, seq_at(k, 0))
            copy.start()
            q_copies[k] = copy

    def attend(xs, s):
        scores = lax.dot_general(
            q[xs], kv[s, :, :HD], (((1,), (1,)), ((), ())), preferred_element_type=F32
        )
        queries = segq[xs]
        same = jnp.concatenate([queries, queries], axis=1) == segk[s, 0:1, :]
        weights = jnp.where(same, jnp.exp2(scores * SCALE), 0.0)
        product = jnp.dot(weights.astype(BF16), kv[s, :, HD:], preferred_element_type=F32)
        lanes = weights[:, :HD] + weights[:, HD:]
        if s == 0:
            numer[xs] = product
            den[xs] = lanes
        else:
            numer[xs] += product
            den[xs] += lanes

    def tokens_in(slots):
        for t in slots:
            token_ring.arrived(t)
            token_ring.go(t)
            token_pair.go(t)

    def project_mine(slots):
        for t in slots:
            project(0, t)

    def project_theirs(slots):
        for t in slots:
            token_pair.arrived(t)
            project(1, t)

    def keys_in(slots):
        for t in slots:
            kv_ring.arrived(t)
            kv_ring.go(t)

    def queries_in():
        for k in range(1, NX):
            q_copies[k].wait_recv()

    def attend_all(places, slots):
        for t in slots:
            for xs in places:
                attend(xs, t)

    def mix(o, s):
        h = dp_at(-s, core if o == 0 else 1 - core)
        weight = wb[lax.rem(x - h - dp + 2 * HEADS, NX), :, h // NX].reshape(HD, FEAT)
        product = jnp.dot(att[o, s], weight, preferred_element_type=F32)
        if (o, s) == (0, 0):
            acc[:, :FEAT] = product
        else:
            acc[:, :FEAT] += product

    def segments():
        loads[3].wait()
        gain32[...] = gainin[...].astype(F32)
        loads[4].wait()
        lane = lax.broadcasted_iota(jnp.int32, (HD, HD), 1)
        row = lax.broadcasted_iota(jnp.int32, (HD, HD), 0)
        lens_lane = jnp.concatenate([lenin[...].astype(F32), jnp.zeros((1, HD - DOCS), F32)], axis=1)
        lens_lane = jnp.broadcast_to(lens_lane, (HD, HD))
        lens_row = jnp.transpose(lens_lane)
        ends_lane = jnp.sum(jnp.where(row <= lane, lens_row, 0.0), axis=0, keepdims=True)
        ends_row = jnp.sum(jnp.where(lane <= row, lens_lane, 0.0), axis=1, keepdims=True)
        for s in range(NX):
            base = seq_at(-s, 0) * ROWS
            position = (lax.broadcasted_iota(jnp.int32, (ROWS, HD), 0) + base).astype(F32)
            count = jnp.sum(jnp.where(position >= ends_lane, 1.0, 0.0), axis=1, keepdims=True)
            segq[s] = jnp.broadcast_to(count, (ROWS, HD))
        for s in range(NZ):
            base = seq_at(0, -s) * ROWS
            position = (lax.broadcasted_iota(jnp.int32, (HD, ROWS), 1) + base).astype(F32)
            count = jnp.sum(jnp.where(position >= ends_row, 1.0, 0.0), axis=0, keepdims=True)
            segk[s] = jnp.broadcast_to(count, (8, ROWS))


    r_copies = {}

    def send_sums(k):
        redo[k] = numer[k].astype(BF16)
        for i in range(ROWS // HD):
            part_sum = jnp.sum(jnp.transpose(den[k, pl.ds(i * HD, HD), :]), axis=0, keepdims=True)
            dedo[k, pl.ds(8 * i, 8), :] = jnp.broadcast_to(part_sum, (8, HD))
        for i, (out_part, in_part) in enumerate(((redo, redi), (dedo, dedi))):
            copy = remote(out_part.at[k], in_part.at[k], rsend.at[i, k], rrecv.at[i, k], dp, seq_at(-k, 0))
            copy.start()
            r_copies[i, k] = copy

    def run():
        start_first()
        token_ring.go(0)
        token_pair.go(0)
        segments()
        loads[5].wait()
        project_mine((0,))
        project_theirs((0,))
        tokens_in((2, 6, 1, 7))
        start_second()
        project_mine((2, 6, 1, 7))
        project_theirs((2, 6, 1, 7))
        tokens_in((3, 5))
        project_mine((3, 5))
        tokens_in((4,))
        project_mine((4,))
        project_theirs((3, 5, 4))
        projected()
        start_third()
        attend(0, 0)
        queries_in()
        attend_all((1, 2, 3), (0,))
        keys_in((2, 6))
        keys_in((1, 7))
        attend_all(range(NX), (2, 6, 1, 7))
        for k in (1, 3):
            weight_ring.arrived(k)
            weight_ring.go(k)
        keys_in((3, 5))
        attend_all(range(NX), (3, 5))
        keys_in((4,))
        for k in (2, 1, 3):
            attend(k, 4)
            send_sums(k)
        attend(0, 4)
        for k in (1, 3, 2):
            for i in range(2):
                r_copies[i, k].wait_recv()
        for c in range(ROWS // HD):
            rows = pl.ds(c * HD, HD)
            down = jnp.sum(jnp.transpose(den[0, rows, :]), axis=0, keepdims=True)
            for k in range(1, NX):
                down = down + dedi[k, pl.ds(8 * c, 8), :][0:1, :]
            down = jnp.transpose(jnp.broadcast_to(down, (HD, HD)))
            top = numer[0, rows, :] + redi[1, rows, :].astype(F32) + redi[2, rows, :].astype(F32)
            top = top + redi[3, rows, :].astype(F32)
            att[0, 0, rows, :] = (top / down).astype(BF16)
        att_ring.go(0)
        att_pair.go(0)
        weight_ring.arrived(2)

        def att_in(slots):
            for t in slots:
                att_ring.arrived(t)
                att_ring.go(t)
                att_pair.go(t)

        def mix_mine(slots):
            for t in slots:
                mix(0, t)

        def mix_theirs(slots):
            for t in slots:
                att_pair.arrived(t)
                mix(1, t)

        mix_mine((0,))
        mix_theirs((0,))
        att_in((2, 6, 1, 7))
        mix_mine((2, 6, 1, 7))
        mix_theirs((2, 6, 1, 7))
        att_in((3, 5))
        mix_mine((3, 5))
        att_in((4,))
        mix_mine((4,))
        mix_theirs((3, 5, 4))
        out[...] = acc[:, :FEAT].astype(BF16)

    run()
    for group in (token_ring, token_pair, kv_ring, att_ring, att_pair, weight_ring):
        group.finish()
    for copy in list(q_copies.values()) + list(r_copies.values()):
        copy.wait_send()

    for i in range(HEADS // NX):
        @pl.when(NX * i + turn != dp)
        def _():
            first_hop(i).wait_send()

    @pl.loop(1, NZ)
    def _(k):
        second_hop(k).wait_send()


def body(tokens, mask_flags, doc_lengths, mask_embed, norm_gain, qkv_weight, out_weight):
    vmem = pl.BlockSpec(memory_space=pltpu.VMEM)
    hbm = pl.BlockSpec(memory_space=pltpu.HBM)
    dma = lambda *shape: pltpu.SemaphoreType.DMA(shape)
    return pl.pallas_call(
        kernel,
        out_shape=jax.ShapeDtypeStruct((ROWS, FEAT), BF16),
        in_specs=[hbm] * 7,
        out_specs=vmem,
        scratch_shapes=[
            pltpu.VMEM((ROWS, FEAT), BF16),
            pltpu.VMEM((ROWS // HD, HD), jnp.int32),
            pltpu.VMEM((1, DOCS), jnp.int32),
            pltpu.VMEM((2, HD), BF16),
            pltpu.VMEM((D // HD, HD), BF16),
            pltpu.VMEM((D // HD, HD), F32),
            pltpu.VMEM((2, NY, ROWS, FEAT), BF16),
            pltpu.VMEM((D, 3 * HD), BF16),
            pltpu.VMEM((NZ, ROWS, 2 * HD), BF16),
            pltpu.VMEM((NX, ROWS, HD), BF16),
            pltpu.VMEM((NX, ROWS, HD), F32),
            pltpu.VMEM((NX, ROWS, HD), F32),
            pltpu.VMEM((NX, ROWS, HD), BF16),
            pltpu.VMEM((NX, ROWS, HD), BF16),
            pltpu.VMEM((NX, 16, HD), F32),
            pltpu.VMEM((NX, 16, HD), F32),
            pltpu.VMEM((2, NY, ROWS, HD), BF16),
            pltpu.VMEM((NX, NZ, HEADS // NX, 16, FEAT), BF16),
            pltpu.VMEM((ROWS, 3 * HD), F32),
            pltpu.VMEM((ROWS, HD), F32),
            pltpu.VMEM((NX, ROWS, HD), F32),
            pltpu.VMEM((NZ, 8, ROWS), F32),
            dma(7),
            dma(9), dma(9), dma(8), dma(8),
            dma(9), dma(9), dma(NX), dma(NX),
            dma(2, NX), dma(2, NX),
            dma(9), dma(9), dma(8), dma(8),
            dma(HEADS // NX), dma(HEADS // NX), dma(NZ), dma(NZ), dma(NX + 1), dma(NX + 1),
        ],
        compiler_params=pltpu.CompilerParams(
            collective_id=0, has_side_effects=True, vmem_limit_bytes=VMEM_BYTES
        ),
        name="attention_layer",
    )(
        tokens, mask_flags.reshape(ROWS // HD, HD), doc_lengths.reshape(1, DOCS), mask_embed.reshape(2, HD),
        norm_gain.reshape(D // HD, HD), qkv_weight.reshape(D, 3 * HD), out_weight,
    )


def solution(mesh):
    placed = (P("seq", "dp"), P("seq"), P(), P("dp"), P(), P(None, "dp", None), P("dp", None, None))
    return jax.shard_map(
        body, mesh=mesh, in_specs=placed, out_specs=P("seq", "dp"), check_vma=False
    )
```

time: 308 us -> 74.3 us (0.24)
  waiting for transfers between devices: 268 us -> 0 us
  Pallas kernels: 0 us -> 72.6 us
  matrix products: 16.7 us -> 0 us
  between operations: 13.2 us -> 0.01 us
  other arithmetic: 7.67 us -> 0 us
    all_gather x3 -> x0, waiting for transfers between devices: 202 us -> none  [the longest x1 77.3 us: body(): value_piece = lax.all_gather(value_rows, 'seq', axis=0, tiled=True)]
    pallas_call x0 -> x1, Pallas kernels: none -> 72.6 us  [body(): pl.pallas_call(kernel, out_shape=jax.ShapeDtypeStruct((ROWS, FEAT), BF16)...]
    reduce_scatter x1 -> x0, waiting for transfers between devices: 65.3 us -> none  [body(): lax.psum_scatter(partial_value, 'dp', scatter_dimension=1, tiled=True)]
    dot_general x3 -> x0, matrix products: 16.7 us -> none  [the longest x1 8.14 us: body(): jnp.einsum('qhd,hdn->qn', attended, out_weight, preferred_element_type=jn...]
  transfers between devices with their start and end apart: 4 -> 0, of which waited for: 4 -> 0; matrix products, arithmetic and copies ran while one was open for 2% -> 0% of each run, Pallas kernels for 0% -> 0%
where the time goes in v2:
time: 74.3 us; the launch traced here: 74.2 us
  Pallas kernels  72.6 us (98%)
  local copies, waits for them, and re-layouts  1.57 us (2%)
    pallas_call x1, Pallas kernels, body(): pl.pallas_call(kernel, out_shape=jax.ShapeDtypeStruct((ROWS, FEAT), BF16)...  72.6 us
    unnamed x1, local copies, waits for them, and re-layouts  1.57 us

profile of v2, /device:TPU:1, one launch (start us, length us, event | category | flops | bytes accessed | tf_op | source)
XLA Modules:
  0.0 74.2 jit_solution(11139286236829826956)
XLA Ops:
  0.0 72.6 %attention_layer.1 = bf16[256,256]{1,0:T(8,128)(2,1)} custom-call(bf16[256,256]{1,0:T(8,128)(2,1)} %tokens.1, s32[2,128]{1,0:T(2,128)} %bitcast.7, s32[1,64]{1,0:T(1,128)} %bitcast.8, bf16[2,128]{1,0:T(2,128)(2,1)} %bitcast.9, bf16[32,128]{1,0:T(8,128)(2,1)} %bitcast.6, bf16[4096,384]{1,0:T(8,128)(2,1)} %bitcast.5, bf16[1,128,4096]{2,1,0:T(8,128)(2,1)} %wout.1), custom_call_target="tpu_custom_call" | custom-call | tf_op jit(solution)/shard_map/attention_layer/pallas_call | solution.py:429
  72.6 1.6 %copy.9 = bf16[256,256]{1,0:T(8,128)(2,1)} copy(bf16[256,256]{1,0:T(8,128)(2,1)} %attention_layer.1) | data formatting | bytes 262144

commit v3 on v2

--- a/solution.py
+++ b/solution.py
@@ -10,7 +10,9 @@
 NY, NX, NZ = 8, 4, 8
 ROWS, FEAT, HD, HEADS, D, DOCS = 256, 256, 128, 16, 4096, 64
 VMEM_BYTES = 63 * 1024 * 1024
-H = ROWS // 2
+NC = 2
+R = ROWS // NC
+H = R // 2
 F32, BF16 = jnp.float32, jnp.bfloat16
 SCALE = math.log2(math.e) / math.sqrt(HD)
 
@@ -38,9 +40,9 @@
         self.plan, self.slot, self.send, self.recv, self.place = plan, slot, send, recv, place
         self.copies = {}
 
-    def go(self, s):
+    def go(self, s, only=None):
         for source, step in self.plan:
-            if source == s:
+            if source == s and (only is None or abs(step) == only):
                 to = (s + step) % self.size
                 half = None if to != self.size // 2 else (0 if step > 0 else 1)
                 sem = self.size if half == 1 else to
@@ -84,7 +86,7 @@
 
 def kernel(
     tokens, flags, lens, embed, gain, wqkv, wout, out,
-    tokin, flagin, lenin, embedin, gainin, gain32, tok, w, kv, q, numer, den, redo, redi, dedo, dedi, att, wb, acc, ssq, segq, segk,
+    tokin, flagin, lenin, embedin, gainin, gain32, tok, w, kv, q, numer, den, redo, redi, att, wb, acc, ssq, segq, segk,
     local, ysend, yrecv, bsend, brecv, zsend, zrecv, qsend, qrecv, rsend, rrecv,
     asend, arecv, csend, crecv, was, war, wbs, wbr, wcs, wcr,
 ):
@@ -146,14 +148,31 @@
     def along_x(step):
         return dp, seq_at(step, 0)
 
-    def rows_of(half):
-        return pl.ds(0, ROWS) if half is None else pl.ds(half * H, H)
-
-    token_ring = Ring(T_PLAN, lambda s, half: tok.at[0, s, rows_of(half)], ysend, yrecv, along_y)
-    token_pair = Pair(lambda s: tok.at[0, s], lambda s: tok.at[1, s], bsend, brecv, sibling)
-    kv_ring = Ring(KV_PLAN, lambda s, half: kv.at[s, rows_of(half)], zsend, zrecv, along_z)
-    att_ring = Ring(ATT_PLAN, lambda s, half: att.at[0, s, rows_of(half)], asend, arecv, along_y)
-    att_pair = Pair(lambda s: att.at[0, s], lambda s: att.at[1, s], csend, crecv, sibling)
+    def part(c, half):
+        return pl.ds(c * R, R) if half is None else pl.ds(c * R + half * H, H)
+
+    token_ring = [
+        Ring(T_PLAN, lambda s, half, c=c: tok.at[0, s, part(c, half)], ysend.at[c], yrecv.at[c], along_y)
+        for c in range(NC)
+    ]
+    token_pair = [
+        Pair(lambda s, c=c: tok.at[0, s, part(c, None)], lambda s, c=c: tok.at[1, s, part(c, None)],
+             bsend.at[c], brecv.at[c], sibling)
+        for c in range(NC)
+    ]
+    kv_ring = [
+        Ring(KV_PLAN, lambda s, half, c=c: kv.at[s, part(c, half)], zsend.at[c], zrecv.at[c], along_z)
+        for c in range(NC)
+    ]
+    att_ring = [
+        Ring(ATT_PLAN, lambda s, half, c=c: att.at[0, s, part(c, half)], asend.at[c], arecv.at[c], along_y)
+        for c in range(NC)
+    ]
+    att_pair = [
+        Pair(lambda s, c=c: att.at[0, s, part(c, None)], lambda s, c=c: att.at[1, s, part(c, None)],
+             csend.at[c], crecv.at[c], sibling)
+        for c in range(NC)
+    ]
 
     def weight_part(s, half):
         return wb.at[s] if half is None else wb.at[s, pl.ds(half * (NZ // 2), NZ // 2)]
@@ -209,9 +228,10 @@
 
         weight_ring.go(0)
 
-    def project(o, s):
+    def project(o, s, c):
+        rows = pl.ds(c * R, R)
         f = dp_at(-s, core if o == 0 else 1 - core)
-        values = tok[o, s].astype(F32)
+        values = tok[o, s, rows, :].astype(F32)
         squares = values * values
         squares = squares[:, :HD] + squares[:, HD:]
         gains = jnp.concatenate([gain32[pl.ds(2 * f, 1), :], gain32[pl.ds(2 * f + 1, 1), :]], axis=1)
@@ -220,78 +240,81 @@
             scaled, w[pl.ds(pl.multiple_of(f * FEAT, FEAT), FEAT), :], preferred_element_type=F32
         )
         if (o, s) == (0, 0):
-            ssq[...] = squares
-            acc[...] = product
+            ssq[rows, :] = squares
+            acc[rows, :] = product
         else:
-            ssq[...] += squares
-            acc[...] += product
+            ssq[rows, :] += squares
+            acc[rows, :] += product
 
     q_copies = {}
 
-    def projected():
-        total = jnp.sum(ssq[...], axis=1, keepdims=True)
+    def projected(c):
+        rows = pl.ds(c * R, R)
+        total = jnp.sum(ssq[rows, :], axis=1, keepdims=True)
         inv_rms = lax.rsqrt(total / D + 1e-05)
-        kv[0] = (acc[:, HD:] * inv_rms).astype(BF16)
-        kv_ring.go(0)
-        q[0] = (acc[:, :HD] * inv_rms).astype(BF16)
+        kv[0, rows, :] = (acc[rows, HD:] * inv_rms).astype(BF16)
+        kv_ring[c].go(0)
+        q[0, rows, :] = (acc[rows, :HD] * inv_rms).astype(BF16)
         for k in (2, 1, 3):
-            copy = remote(q.at[0], q.at[k], qsend.at[k], qrecv.at[k], dp, seq_at(k, 0))
+            copy = remote(q.at[0, rows], q.at[k, rows], qsend.at[c, k], qrecv.at[c, k], dp, seq_at(k, 0))
             copy.start()
-            q_copies[k] = copy
-
-    def attend(xs, s):
+            q_copies[c, k] = copy
+
+    def attend(places, rows, s, c):
+        keys = pl.ds(c * R, R)
+        queries = q[places, rows, :]
+        shape = queries.shape
         scores = lax.dot_general(
-            q[xs], kv[s, :, :HD], (((1,), (1,)), ((), ())), preferred_element_type=F32
+            queries.reshape(-1, HD), kv[s, keys, :HD], (((1,), (1,)), ((), ())), preferred_element_type=F32
         )
-        queries = segq[xs]
-        same = jnp.concatenate([queries, queries], axis=1) == segk[s, 0:1, :]
+        same = segq[places, rows, :].reshape(-1, HD) == segk[s, 0:1, keys]
         weights = jnp.where(same, jnp.exp2(scores * SCALE), 0.0)
-        product = jnp.dot(weights.astype(BF16), kv[s, :, HD:], preferred_element_type=F32)
-        lanes = weights[:, :HD] + weights[:, HD:]
-        if s == 0:
-            numer[xs] = product
-            den[xs] = lanes
+        product = jnp.dot(weights.astype(BF16), kv[s, keys, HD:], preferred_element_type=F32)
+        if (s, c) == (0, 0):
+            numer[places, rows, :] = product.reshape(shape)
+            den[places, rows, :] = weights.reshape(shape)
         else:
-            numer[xs] += product
-            den[xs] += lanes
-
-    def tokens_in(slots):
+            numer[places, rows, :] += product.reshape(shape)
+            den[places, rows, :] += weights.reshape(shape)
+
+    def tokens_in(c, slots):
         for t in slots:
-            token_ring.arrived(t)
-            token_ring.go(t)
-            token_pair.go(t)
-
-    def project_mine(slots):
+            token_ring[c].arrived(t)
+            token_ring[c].go(t)
+            token_pair[c].go(t)
+
+    def project_mine(c, slots):
         for t in slots:
-            project(0, t)
-
-    def project_theirs(slots):
+            project(0, t, c)
+
+    def project_theirs(c, slots):
         for t in slots:
-            token_pair.arrived(t)
-            project(1, t)
-
-    def keys_in(slots):
+            token_pair[c].arrived(t)
+            project(1, t, c)
+
+    def keys_in(c, slots):
         for t in slots:
-            kv_ring.arrived(t)
-            kv_ring.go(t)
-
-    def queries_in():
+            kv_ring[c].arrived(t)
+            kv_ring[c].go(t)
+
+    def queries_in(c):
         for k in range(1, NX):
-            q_copies[k].wait_recv()
-
-    def attend_all(places, slots):
+            q_copies[c, k].wait_recv()
+
+    def attend_all(chunks, slots, c):
         for t in slots:
-            for xs in places:
-                attend(xs, t)
-
-    def mix(o, s):
+            for qc in chunks:
+                attend(slice(None), pl.ds(qc * R, R), t, c)
+
+    def mix(o, s, c):
+        rows = pl.ds(c * R, R)
         h = dp_at(-s, core if o == 0 else 1 - core)
         weight = wb[lax.rem(x - h - dp + 2 * HEADS, NX), :, h // NX].reshape(HD, FEAT)
-        product = jnp.dot(att[o, s], weight, preferred_element_type=F32)
+        product = jnp.dot(att[o, s, rows, :], weight, preferred_element_type=F32)
         if (o, s) == (0, 0):
-            acc[:, :FEAT] = product
+            acc[rows, :FEAT] = product
         else:
-            acc[:, :FEAT] += product
+            acc[rows, :FEAT] += product
 
     def segments():
         loads[3].wait()
@@ -318,85 +341,126 @@
 
     r_copies = {}
 
-    def send_sums(k):
-        redo[k] = numer[k].astype(BF16)
-        for i in range(ROWS // HD):
-            part_sum = jnp.sum(jnp.transpose(den[k, pl.ds(i * HD, HD), :]), axis=0, keepdims=True)
-            dedo[k, pl.ds(8 * i, 8), :] = jnp.broadcast_to(part_sum, (8, HD))
-        for i, (out_part, in_part) in enumerate(((redo, redi), (dedo, dedi))):
-            copy = remote(out_part.at[k], in_part.at[k], rsend.at[i, k], rrecv.at[i, k], dp, seq_at(-k, 0))
-            copy.start()
-            r_copies[i, k] = copy
+    def send_sums(k, c):
+        rows = pl.ds(c * R, R)
+        redo[k, c, :R, :] = numer[k, rows, :].astype(BF16)
+        left = jnp.sum(jnp.transpose(den[k, rows, :]), axis=0, keepdims=True)
+        at = lax.broadcasted_iota(jnp.int32, (16, HD), 0)
+        terms = jnp.zeros((16, HD), F32)
+        for i in range(3):
+            term = left.astype(BF16).astype(F32)
+            terms = jnp.where(at == i, term, terms)
+            left = left - term
+        redo[k, c, R:, :] = terms.astype(BF16)
+        copy = remote(redo.at[k, c], redi.at[k, c], rsend.at[c, k], rrecv.at[c, k], dp, seq_at(-k, 0))
+        copy.start()
+        r_copies[c, k] = copy
+
+    def combine(c):
+        rows = pl.ds(c * R, R)
+        down = jnp.sum(jnp.transpose(den[0, rows, :]), axis=0, keepdims=True)
+        top = numer[0, rows, :]
+        for k in (1, 3, 2):
+            r_copies[c, k].wait_recv()
+            top = top + redi[k, c, :R, :].astype(F32)
+            terms = redi[k, c, R:, :].astype(F32)
+            down = down + (terms[0:1, :] + terms[1:2, :] + terms[2:3, :])
+        down = jnp.transpose(jnp.broadcast_to(down, (HD, HD)))
+        att[0, 0, rows, :] = (top / down).astype(BF16)
+        att_ring[c].go(0)
+        att_pair[c].go(0)
 
     def run():
         start_first()
-        token_ring.go(0)
-        token_pair.go(0)
+        token_ring[0].go(0)
+        token_ring[1].go(0, only=2)
+        for c in range(NC):
+            token_pair[c].go(0)
         segments()
         loads[5].wait()
-        project_mine((0,))
-        project_theirs((0,))
-        tokens_in((2, 6, 1, 7))
+        project_mine(0, (0,))
+        project_theirs(0, (0,))
+        tokens_in(0, (2, 6))
+        token_ring[1].go(0, only=1)
+        tokens_in(0, (1, 7))
         start_second()
-        project_mine((2, 6, 1, 7))
-        project_theirs((2, 6, 1, 7))
-        tokens_in((3, 5))
-        project_mine((3, 5))
-        tokens_in((4,))
-        project_mine((4,))
-        project_theirs((3, 5, 4))
-        projected()
+        project_mine(0, (2, 6, 1, 7))
+        project_theirs(0, (2, 6, 1, 7))
+        tokens_in(1, (2, 6))
+        tokens_in(0, (3, 5))
+        project_mine(0, (3, 5))
+        tokens_in(0, (4,))
+        project_mine(0, (4,))
+        project_theirs(0, (3, 5, 4))
+        projected(0)
+        tokens_in(1, (1, 7))
+        project_mine(1, (0, 2, 6, 1, 7))
+        project_theirs(1, (0, 2, 6, 1, 7))
+        tokens_in(1, (3, 5))
+        project_mine(1, (3, 5))
+        tokens_in(1, (4,))
+        project_mine(1, (4,))
+        project_theirs(1, (3, 5, 4))
+        projected(1)
         start_third()
-        attend(0, 0)
-        queries_in()
-        attend_all((1, 2, 3), (0,))
-        keys_in((2, 6))
-        keys_in((1, 7))
-        attend_all(range(NX), (2, 6, 1, 7))
+        keys_in(0, (2, 6))
+        queries_in(0)
+        attend_all((0,), (0,), 0)
+        keys_in(0, (1, 7))
+        attend_all((0,), (2, 6, 1, 7), 0)
+        keys_in(0, (3, 5))
+        attend_all((0,), (3, 5), 0)
+        keys_in(1, (2, 6))
+        queries_in(1)
+        attend_all((1,), (0, 2, 6, 1, 7, 3, 5), 0)
+        attend_all((0, 1), (0,), 1)
+        keys_in(0, (4,))
+        attend_all((0, 1), (4,), 0)
+        keys_in(1, (1, 7))
+        attend_all((0, 1), (2, 6, 1, 7), 1)
         for k in (1, 3):
             weight_ring.arrived(k)
             weight_ring.go(k)
-        keys_in((3, 5))
-        attend_all(range(NX), (3, 5))
-        keys_in((4,))
-        for k in (2, 1, 3):
-            attend(k, 4)
-            send_sums(k)
-        attend(0, 4)
-        for k in (1, 3, 2):
-            for i in range(2):
-                r_copies[i, k].wait_recv()
-        for c in range(ROWS // HD):
-            rows = pl.ds(c * HD, HD)
-            down = jnp.sum(jnp.transpose(den[0, rows, :]), axis=0, keepdims=True)
-            for k in range(1, NX):
-                down = down + dedi[k, pl.ds(8 * c, 8), :][0:1, :]
-            down = jnp.transpose(jnp.broadcast_to(down, (HD, HD)))
-            top = numer[0, rows, :] + redi[1, rows, :].astype(F32) + redi[2, rows, :].astype(F32)
-            top = top + redi[3, rows, :].astype(F32)
-            att[0, 0, rows, :] = (top / down).astype(BF16)
-        att_ring.go(0)
-        att_pair.go(0)
+        for group in (*token_ring, *token_pair):
+            group.finish()
+        keys_in(1, (3, 5))
+        attend_all((0, 1), (3, 5), 1)
+        keys_in(1, (4,))
+        for c in range(NC):
+            for k in (2, 1, 3):
+                attend(k, pl.ds(c * R, R), 4, 1)
+                send_sums(k, c)
+        attend(0, pl.ds(0, ROWS), 4, 1)
+        for group in kv_ring:
+            group.finish()
+        for copy in q_copies.values():
+            copy.wait_send()
+        for c in range(NC):
+            combine(c)
         weight_ring.arrived(2)
 
         def att_in(slots):
-            for t in slots:
-                att_ring.arrived(t)
-                att_ring.go(t)
-                att_pair.go(t)
+            for c in range(NC):
+                for t in slots:
+                    att_ring[c].arrived(t)
+                    att_ring[c].go(t)
+                    att_pair[c].go(t)
 
         def mix_mine(slots):
-            for t in slots:
-                mix(0, t)
+            for c in range(NC):
+                for t in slots:
+                    mix(0, t, c)
 
         def mix_theirs(slots):
-            for t in slots:
-                att_pair.arrived(t)
-                mix(1, t)
+            for c in range(NC):
+                for t in slots:
+                    att_pair[c].arrived(t)
+                    mix(1, t, c)
 
         mix_mine((0,))
+        att_in((2, 6))
         mix_theirs((0,))
-        att_in((2, 6, 1, 7))
+        att_in((1, 7))
         mix_mine((2, 6, 1, 7))
         mix_theirs((2, 6, 1, 7))
         att_in((3, 5))
@@ -407,9 +471,9 @@
         out[...] = acc[:, :FEAT].astype(BF16)
 
     run()
-    for group in (token_ring, token_pair, kv_ring, att_ring, att_pair, weight_ring):
+    for group in (*att_ring, *att_pair, weight_ring):
         group.finish()
-    for copy in list(q_copies.values()) + list(r_copies.values()):
+    for copy in r_copies.values():
         copy.wait_send()
 
     for i in range(HEADS // NX):
@@ -444,10 +508,8 @@
             pltpu.VMEM((NX, ROWS, HD), BF16),
             pltpu.VMEM((NX, ROWS, HD), F32),
             pltpu.VMEM((NX, ROWS, HD), F32),
-            pltpu.VMEM((NX, ROWS, HD), BF16),
-            pltpu.VMEM((NX, ROWS, HD), BF16),
-            pltpu.VMEM((NX, 16, HD), F32),
-            pltpu.VMEM((NX, 16, HD), F32),
+            pltpu.VMEM((NX, NC, R + 16, HD), BF16),
+            pltpu.VMEM((NX, NC, R + 16, HD), BF16),
             pltpu.VMEM((2, NY, ROWS, HD), BF16),
             pltpu.VMEM((NX, NZ, HEADS // NX, 16, FEAT), BF16),
             pltpu.VMEM((ROWS, 3 * HD), F32),
@@ -455,10 +517,10 @@
             pltpu.VMEM((NX, ROWS, HD), F32),
             pltpu.VMEM((NZ, 8, ROWS), F32),
             dma(7),
-            dma(9), dma(9), dma(8), dma(8),
-            dma(9), dma(9), dma(NX), dma(NX),
-            dma(2, NX), dma(2, NX),
-            dma(9), dma(9), dma(8), dma(8),
+            dma(NC, 9), dma(NC, 9), dma(NC, 8), dma(NC, 8),
+            dma(NC, 9), dma(NC, 9), dma(NC, NX), dma(NC, NX),
+            dma(NC, NX), dma(NC, NX),
+            dma(NC, 9), dma(NC, 9), dma(NC, 8), dma(NC, 8),
             dma(HEADS // NX), dma(HEADS // NX), dma(NZ), dma(NZ), dma(NX + 1), dma(NX + 1),
         ],
         compiler_params=pltpu.CompilerParams(

time: 74.3 us -> 72.1 us (0.970)
  Pallas kernels: 72.6 us -> 70.4 us
    pallas_call x1, Pallas kernels: 72.6 us -> 70.4 us  [body(): pl.pallas_call(kernel, out_shape=jax.ShapeDtypeStruct((ROWS, FEAT), BF16)...]
where the time goes in v3:
time: 72.1 us; the launch traced here: 72 us
  Pallas kernels  70.4 us (98%)
  local copies, waits for them, and re-layouts  1.57 us (2%)
    pallas_call x1, Pallas kernels, body(): pl.pallas_call(kernel, out_shape=jax.ShapeDtypeStruct((ROWS, FEAT), BF16)...  70.4 us
    unnamed x1, local copies, waits for them, and re-layouts  1.57 us

profile of v3, /device:TPU:1, one launch (start us, length us, event | category | flops | bytes accessed | tf_op | source)
XLA Modules:
  0.0 72.0 jit_solution(3653117233615650113)
XLA Ops:
  0.0 70.4 %attention_layer.1 = bf16[256,256]{1,0:T(8,128)(2,1)} custom-call(bf16[256,256]{1,0:T(8,128)(2,1)} %tokens.1, s32[2,128]{1,0:T(2,128)} %bitcast.7, s32[1,64]{1,0:T(1,128)} %bitcast.8, bf16[2,128]{1,0:T(2,128)(2,1)} %bitcast.9, bf16[32,128]{1,0:T(8,128)(2,1)} %bitcast.6, bf16[4096,384]{1,0:T(8,128)(2,1)} %bitcast.5, bf16[1,128,4096]{2,1,0:T(8,128)(2,1)} %wout.1), custom_call_target="tpu_custom_call" | custom-call | tf_op jit(solution)/shard_map/attention_layer/pallas_call | solution.py:493
  70.4 1.6 %copy.9 = bf16[256,256]{1,0:T(8,128)(2,1)} copy(bf16[256,256]{1,0:T(8,128)(2,1)} %attention_layer.1) | data formatting | bytes 262144

commit v4 on v3

--- a/solution.py
+++ b/solution.py
@@ -25,12 +25,7 @@
 
 
 CROSS = ((0, 1), (0, -1), (1, 1), (3, -1))
-TREE = ((0, 2), (0, -2), (0, 1), (0, -1), (2, 2), (6, -2), (2, 1), (6, -1))
-
-
-T_PLAN = TREE
-KV_PLAN = TREE
-ATT_PLAN = TREE
+TREE = ((0, 2), (0, -2), (0, 1), (0, -1), (2, 1), (6, -1), (2, 2), (6, -2))
 
 
 class Ring:
@@ -152,7 +147,7 @@
         return pl.ds(c * R, R) if half is None else pl.ds(c * R + half * H, H)
 
     token_ring = [
-        Ring(T_PLAN, lambda s, half, c=c: tok.at[0, s, part(c, half)], ysend.at[c], yrecv.at[c], along_y)
+        Ring(TREE, lambda s, half, c=c: tok.at[0, s, part(c, half)], ysend.at[c], yrecv.at[c], along_y)
         for c in range(NC)
     ]
     token_pair = [
@@ -161,11 +156,11 @@
         for c in range(NC)
     ]
     kv_ring = [
-        Ring(KV_PLAN, lambda s, half, c=c: kv.at[s, part(c, half)], zsend.at[c], zrecv.at[c], along_z)
+        Ring(TREE, lambda s, half, c=c: kv.at[s, part(c, half)], zsend.at[c], zrecv.at[c], along_z)
         for c in range(NC)
     ]
     att_ring = [
-        Ring(ATT_PLAN, lambda s, half, c=c: att.at[0, s, part(c, half)], asend.at[c], arecv.at[c], along_y)
+        Ring(TREE, lambda s, half, c=c: att.at[0, s, part(c, half)], asend.at[c], arecv.at[c], along_y)
         for c in range(NC)
     ]
     att_pair = [
@@ -220,6 +215,16 @@
         @pl.loop(1, NZ)
         def _(k):
             second_hop(k).start()
+
+    def finish_hops():
+        for i in range(HEADS // NX):
+            @pl.when(NX * i + turn != dp)
+            def _():
+                first_hop(i).wait_send()
+
+        @pl.loop(1, NZ)
+        def _(k):
+            second_hop(k).wait_send()
 
     def start_third():
         @pl.loop(1, NZ)
@@ -408,9 +413,9 @@
         attend_all((0,), (0,), 0)
         keys_in(0, (1, 7))
         attend_all((0,), (2, 6, 1, 7), 0)
+        keys_in(1, (2, 6))
         keys_in(0, (3, 5))
         attend_all((0,), (3, 5), 0)
-        keys_in(1, (2, 6))
         queries_in(1)
         attend_all((1,), (0, 2, 6, 1, 7, 3, 5), 0)
         attend_all((0, 1), (0,), 1)
@@ -458,6 +463,10 @@
                     mix(1, t, c)
 
         mix_mine((0,))
+        for copy in r_copies.values():
+            copy.wait_send()
+        weight_ring.finish()
+        finish_hops()
         att_in((2, 6))
         mix_theirs((0,))
         att_in((1, 7))
@@ -467,23 +476,14 @@
         mix_mine((3, 5))
         att_in((4,))
         mix_mine((4,))
+        for group in att_ring:
+            group.finish()
         mix_theirs((3, 5, 4))
         out[...] = acc[:, :FEAT].astype(BF16)
 
     run()
-    for group in (*att_ring, *att_pair, weight_ring):
+    for group in att_pair:
         group.finish()
-    for copy in r_copies.values():
-        copy.wait_send()
-
-    for i in range(HEADS // NX):
-        @pl.when(NX * i + turn != dp)
-        def _():
-            first_hop(i).wait_send()
-
-    @pl.loop(1, NZ)
-    def _(k):
-        second_hop(k).wait_send()
 
 
 def body(tokens, mask_flags, doc_lengths, mask_embed, norm_gain, qkv_weight, out_weight):

time: 72.1 us -> 70.2 us (0.974)
  Pallas kernels: 70.4 us -> 68.5 us
    pallas_call x1, Pallas kernels: 70.4 us -> 68.5 us  [body(): pl.pallas_call(kernel, out_shape=jax.ShapeDtypeStruct((ROWS, FEAT), BF16)...]
where the time goes in v4:
time: 70.2 us; the launch traced here: 70.1 us
  Pallas kernels  68.5 us (98%)
  local copies, waits for them, and re-layouts  1.57 us (2%)
    pallas_call x1, Pallas kernels, body(): pl.pallas_call(kernel, out_shape=jax.ShapeDtypeStruct((ROWS, FEAT), BF16)...  68.5 us
    unnamed x1, local copies, waits for them, and re-layouts  1.57 us

profile of v4, /device:TPU:1, one launch (start us, length us, event | category | flops | bytes accessed | tf_op | source)
XLA Modules:
  0.0 70.1 jit_solution(9195945381462897187)
XLA Ops:
  0.0 68.5 %attention_layer.1 = bf16[256,256]{1,0:T(8,128)(2,1)} custom-call(bf16[256,256]{1,0:T(8,128)(2,1)} %tokens.1, s32[2,128]{1,0:T(2,128)} %bitcast.7, s32[1,64]{1,0:T(1,128)} %bitcast.8, bf16[2,128]{1,0:T(2,128)(2,1)} %bitcast.9, bf16[32,128]{1,0:T(8,128)(2,1)} %bitcast.6, bf16[4096,384]{1,0:T(8,128)(2,1)} %bitcast.5, bf16[1,128,4096]{2,1,0:T(8,128)(2,1)} %wout.1), custom_call_target="tpu_custom_call" | custom-call | tf_op jit(solution)/shard_map/attention_layer/pallas_call | solution.py:493
  68.5 1.6 %copy.9 = bf16[256,256]{1,0:T(8,128)(2,1)} copy(bf16[256,256]{1,0:T(8,128)(2,1)} %attention_layer.1) | data formatting | bytes 262144

commit v5 on v4

--- a/solution.py
+++ b/solution.py
@@ -95,8 +95,6 @@
             [(tokens, tokin), (flags, flagin), (embed, embedin), (gain, gainin), (lens, lenin), (wqkv, w)]
         )
     ]
-    for load in loads:
-        load.start()
 
     def dp_at(dy, c):
         return lax.rem(y + dy + NY, NY) * 2 + c
@@ -120,6 +118,8 @@
     def _(k):
         pl.semaphore_signal(barrier, inc=1, device_id=(dp, seq_at(k, 0)), device_id_type=pl.DeviceIdType.MESH)
 
+    for load in loads:
+        load.start()
     for load in loads[:3]:
         load.wait()
     embed_row = jnp.concatenate([embedin[0:1, :], embedin[1:2, :]], axis=1).astype(F32)
@@ -432,10 +432,9 @@
         attend_all((0, 1), (3, 5), 1)
         keys_in(1, (4,))
         for c in range(NC):
+            attend_all((c,), (4,), 1)
             for k in (2, 1, 3):
-                attend(k, pl.ds(c * R, R), 4, 1)
                 send_sums(k, c)
-        attend(0, pl.ds(0, ROWS), 4, 1)
         for group in kv_ring:
             group.finish()
         for copy in q_copies.values():

time: 70.2 us -> 69.8 us (level)
  no operation moved by 1% of the time
where the time goes in v5:
time: 69.8 us; the launch traced here: 69.7 us
  Pallas kernels  68.1 us (98%)
  local copies, waits for them, and re-layouts  1.57 us (2%)
    pallas_call x1, Pallas kernels, body(): pl.pallas_call(kernel, out_shape=jax.ShapeDtypeStruct((ROWS, FEAT), BF16)...  68.1 us
    unnamed x1, local copies, waits for them, and re-layouts  1.57 us

profile of v5, /device:TPU:1, one launch (start us, length us, event | category | flops | bytes accessed | tf_op | source)
XLA Modules:
  0.0 69.7 jit_solution(14444232819926327704)
XLA Ops:
  0.0 68.1 %attention_layer.1 = bf16[256,256]{1,0:T(8,128)(2,1)} custom-call(bf16[256,256]{1,0:T(8,128)(2,1)} %tokens.1, s32[2,128]{1,0:T(2,128)} %bitcast.7, s32[1,64]{1,0:T(1,128)} %bitcast.8, bf16[2,128]{1,0:T(2,128)(2,1)} %bitcast.9, bf16[32,128]{1,0:T(8,128)(2,1)} %bitcast.6, bf16[4096,384]{1,0:T(8,128)(2,1)} %bitcast.5, bf16[1,128,4096]{2,1,0:T(8,128)(2,1)} %wout.1), custom_call_target="tpu_custom_call" | custom-call | tf_op jit(solution)/shard_map/attention_layer/pallas_call | solution.py:492
  68.1 1.6 %copy.9 = bf16[256,256]{1,0:T(8,128)(2,1)} copy(bf16[256,256]{1,0:T(8,128)(2,1)} %attention_layer.1) | data formatting | bytes 262144

commit v6 on v5

--- a/solution.py
+++ b/solution.py
@@ -498,7 +498,7 @@
             pltpu.VMEM((ROWS, FEAT), BF16),
             pltpu.VMEM((ROWS // HD, HD), jnp.int32),
             pltpu.VMEM((1, DOCS), jnp.int32),
-            pltpu.VMEM((2, HD), BF16),
+            pltpu.VMEM((2, HD), F32),
             pltpu.VMEM((D // HD, HD), BF16),
             pltpu.VMEM((D // HD, HD), F32),
             pltpu.VMEM((2, NY, ROWS, FEAT), BF16),
@@ -527,7 +527,7 @@
         ),
         name="attention_layer",
     )(
-        tokens, mask_flags.reshape(ROWS // HD, HD), doc_lengths.reshape(1, DOCS), mask_embed.reshape(2, HD),
+        tokens, mask_flags.reshape(ROWS // HD, HD), doc_lengths.reshape(1, DOCS), mask_embed.astype(F32).reshape(2, HD),
         norm_gain.reshape(D // HD, HD), qkv_weight.reshape(D, 3 * HD), out_weight,
     )
 

time: 69.8 us -> 71.2 us (1.020)
  other arithmetic: 0 us -> 1.22 us
    reshape x0 -> x1, other arithmetic: none -> 1.22 us  [body(): mask_embed.astype(F32).reshape(2, HD)]
where the time goes in v6:
time: 71.2 us; the launch traced here: 71 us
  Pallas kernels  68.2 us (96%)
  local copies, waits for them, and re-layouts  1.57 us (2%)
  other arithmetic  1.22 us (2%)
    pallas_call x1, Pallas kernels, body(): pl.pallas_call(kernel, out_shape=jax.ShapeDtypeStruct((ROWS, FEAT), BF16)...  68.2 us
    unnamed x1, local copies, waits for them, and re-layouts  1.57 us

profile of v6, /device:TPU:1, one launch (start us, length us, event | category | flops | bytes accessed | tf_op | source)
XLA Modules:
  0.0 71.0 jit_solution(12496169075947359582)
XLA Ops:
  0.0 1.2 %bitcast_convert_fusion.embed = f32[2,128]{1,0:T(2,128)} fusion(bf16[256]{0:T(256)(128)(2,1)} %param.10), kind=kLoop, calls=%fused_computation | loop fusion | flops 256 | bytes 1536 | tf_op jit(solution)/shard_map/reshape | solution.py:530
  1.2 68.2 %attention_layer.1 = bf16[256,256]{1,0:T(8,128)(2,1)} custom-call(bf16[256,256]{1,0:T(8,128)(2,1)} %tokens.1, s32[2,128]{1,0:T(2,128)} %bitcast.9, s32[1,64]{1,0:T(1,128)} %bitcast.10, f32[2,128]{1,0:T(2,128)} %bitcast_convert_fusion.embed, bf16[32,128]{1,0:T(8,128)(2,1)} %bitcast.8, bf16[4096,384]{1,0:T(8,128)(2,1)} %bitcast.7, bf16[1,128,4096]{2,1,0:T(8,128)(2,1)} %wout.1), custom_call_target="tpu_custom_call" | custom-call | tf_op jit(solution)/shard_map/attention_layer/pallas_call | solution.py:492
  69.4 1.6 %copy.9 = bf16[256,256]{1,0:T(8,128)(2,1)} copy(bf16[256,256]{1,0:T(8,128)(2,1)} %attention_layer.1) | data formatting | bytes 262144
